TPU v7x, 32 devices: a whole 2x2x4 slice. The times are simulated.
32 devices in a mesh: gx: 4 (over y, core), gy: 4 (over z), gz: 2 (over x).
Axes of the slice: x: 2, y: 2, z: 4, core: 2. Of those that a mesh axis runs over, the one named last changes fastest.
Arguments:
- initial_thermal_state: float32 [256, 128, 256], P('gx', 'gy', 'gz'), may hold values from -6 to 6
- thermal_spread_rate: float32 [256, 128, 256], P('gx', 'gy', 'gz'), may hold values from 0.25 to 4
- yz_skew_factor: bfloat16 [256, 128, 256], P('gx', 'gy', 'gz'), may hold values from -1 to 1
Outputs:
- known_source_vector: float32 [256, 128, 256], P('gx', 'gy', 'gz')
- half_step: float32 [256, 128, 256], P('gx', 'gy', 'gz')
All inputs are finite; a program needn't handle non-finite values.
Results may differ from a plain program's by a relative error of at most 0.0003.
Values sent between devices are 32-bit elements; how exact they have to be, the bound alone decides.
A program may use at most 64 MiB of HBM per device.

v0:
```python
import functools
import math

import jax
import jax.numpy as jnp
from jax import lax
from jax.experimental import pallas as pl
from jax.experimental.pallas import tpu as pltpu
from jax.sharding import PartitionSpec as P

ratio_x = 4096.0
ratio_y = 0.2
ratio_z = 0.2
ratio_mix = 0.25
VMEM1 = 61 * 1024 * 1024 + 512 * 1024
VMEM2 = 48 * 1024 * 1024
MESH = pl.DeviceIdType.MESH


def inverse(x):
    guess = pl.reciprocal(x, approx=True)
    guess = guess * (2.0 - x * guess)
    return guess * (2.0 - x * guess)


def link(first, second):
    t1, z1, c1 = first
    t2, z2, c2 = second
    share = inverse(1.0 + z1 * c2)
    k1 = t1 * share
    k2 = t2 * share
    return (k1 * t2, z2 + k2 * t2 * z1, c1 + k1 * t1 * c2), (k1, k2)


def link_sides(weights, first, first_pq, second, second_pq):
    k1, k2 = weights
    p1, q1 = first_pq
    p2, q2 = second_pq
    return (p2 + k2 * (p1 - first[1] * q2), q1 + k1 * (q2 + second[2] * p1))


def pick(flag, yes, no):
    return tuple(jnp.where(flag, s, t) for s, t in zip(yes, no))


def kernel(
    nx, ny, nz, u_hbm, d_hbm, k_hbm, r_buf, rho, start,
    u_pad, d_pad, u_next, u_prev, d_next, d_prev, skew,
    x_halo, y_send, y_recv, z_send, z_recv, own_edge, skew_edge, bend_rows,
    map_send, map_recv, pq_send, pq_recv, rel_send, rel_recv,
    load_sem, halo_send, halo_recv, line_send, line_recv,
):
    planes, rows, lanes = u_hbm.shape
    stages = int(math.log2(nx))
    gx, gy, gz = lax.axis_index("gx"), lax.axis_index("gy"), lax.axis_index("gz")
    other_z = 1 - gz
    pitch = rows + 16
    body_rows = pl.ds(8, rows)
    u_flat = u_pad.reshape(planes * pitch, lanes)
    d_flat = d_pad.reshape(planes * pitch, lanes)

    d_load = pltpu.make_async_copy(d_hbm, d_pad.at[:, body_rows, :], load_sem.at[0])
    u_load = pltpu.make_async_copy(u_hbm, u_pad.at[:, body_rows, :], load_sem.at[1])
    k_load = pltpu.make_async_copy(k_hbm, skew, load_sem.at[2])
    d_load.start()
    u_load.start()
    k_load.start()

    barrier = pltpu.get_barrier_semaphore()

    def greet(x, y, z):
        pl.semaphore_signal(barrier, inc=1, device_id=(x, y, z), device_id_type=MESH)

    partners = [gx + (1 << s) - 2 * (1 << s) * ((gx // (1 << s)) % 2) for s in range(stages)]
    for x in partners:
        greet(x, gy, gz)
    greet(gx, gy, other_z)

    @pl.when(gx > 0)
    def _():
        greet(gx - 1, gy, gz)

    @pl.when(gy > 0)
    def _():
        greet(gx, gy - 1, gz)
        greet(gx, gy - 1, other_z)

    @pl.when(gy < ny - 1)
    def _():
        greet(gx, gy + 1, gz)
        greet(gx, gy + 1, other_z)

    one = jnp.int32(1)
    zero = jnp.int32(0)
    awaited = (
        stages + 1
        + jnp.where(gx < nx - 1, one, zero)
        + 2 * jnp.where(gy > 0, one, zero)
        + 2 * jnp.where(gy < ny - 1, one, zero)
    )

    def remote(src, dst, send, recv, x, y, z):
        return pltpu.make_async_remote_copy(
            src_ref=src, dst_ref=dst, send_sem=send, recv_sem=recv,
            device_id=(x, y, z), device_id_type=MESH,
        )

    x_copy = remote(
        d_hbm.at[planes - 1], x_halo, halo_send.at[0], halo_recv.at[0], gx + 1, gy, gz
    )
    up_copy, down_copy = [
        [
            remote(
                y_send.at[way, field], y_recv.at[1 - way, field],
                halo_send.at[4 + 2 * way + field], halo_recv.at[4 + 2 * way + field], gx, y, gz,
            )
            for field in range(2)
        ]
        for way, y in ((0, gy - 1), (1, gy + 1))
    ]
    z_copy = remote(
        z_send, z_recv.at[:, pl.ds(8, rows), :], halo_send.at[1], halo_recv.at[1], gx, gy, other_z
    )
    up_corner = remote(
        z_send.at[0, pl.ds(0, 8), :], z_recv.at[0, pl.ds(8 + rows, 8), :],
        halo_send.at[2], halo_recv.at[2], gx, gy - 1, other_z,
    )
    down_corner = remote(
        z_send.at[0, pl.ds(rows - 8, 8), :], z_recv.at[0, pl.ds(0, 8), :],
        halo_send.at[3], halo_recv.at[3], gx, gy + 1, other_z,
    )

    @pl.when(gx == 0)
    def _():
        x_halo[...] = jnp.zeros((rows, lanes), jnp.float32)

    @pl.when(gy == 0)
    def _():
        y_recv[0] = jnp.zeros((2, planes, lanes), jnp.float32)
        z_recv[0, 0:8, :] = jnp.zeros((8, lanes), jnp.float32)

    @pl.when(gy == ny - 1)
    def _():
        y_recv[1] = jnp.zeros((2, planes, lanes), jnp.float32)
        z_recv[0, 8 + rows : 16 + rows, :] = jnp.zeros((8, lanes), jnp.float32)

    assert 2 * planes <= lanes and nz == 2
    lane = lax.broadcasted_iota(jnp.int32, (rows, lanes), 1)
    owner = lax.rem((lane + 1) // 2, jnp.int32(planes))

    zeros = jnp.zeros((rows, lanes), jnp.float32)
    ones = jnp.ones((rows, lanes), jnp.float32)

    def gather_edge(i, acc):
        heat = pltpu.roll(u_pad[i, 8 : 8 + rows, :], 2 * i, 1)
        diff = pltpu.roll(d_pad[i, 8 : 8 + rows, :], 2 * i, 1)
        mine = owner == i
        return (jnp.where(mine, heat, acc[0]), jnp.where(mine, diff, acc[1]))

    for field, load, flat in ((1, d_load, d_flat), (0, u_load, u_flat)):
        load.wait()
        y_send[0, field] = flat[pl.ds(8, planes, stride=pitch), :]
        y_send[1, field] = flat[pl.ds(7 + rows, planes, stride=pitch), :]
        if field:
            pl.semaphore_wait(barrier, awaited)

            @pl.when(gx < nx - 1)
            def _():
                x_copy.start()

        @pl.when(gy > 0)
        def _():
            up_copy[field].start()

        @pl.when(gy < ny - 1)
        def _():
            down_copy[field].start()

    edge_heat, edge_diff = lax.fori_loop(0, planes, gather_edge, (zeros, zeros), unroll=8)
    z_send[0] = edge_heat
    z_send[1] = edge_diff

    z_copy.start()

    @pl.when(gy > 0)
    def _():
        up_corner.start()

    @pl.when(gy < ny - 1)
    def _():
        down_corner.start()

    k_load.wait()

    def homogeneous(i, state):
        a, b, c, d, before, acc = state
        here = d_pad[i, 8 : 8 + rows, :]
        heat = u_pad[i, 8 : 8 + rows, :]
        u_next[i, 8 : 8 + rows, :] = pltpu.roll(heat, lanes - 1, 1)
        u_prev[i, 8 : 8 + rows, :] = pltpu.roll(heat, 1, 1)
        d_next[i] = pltpu.roll(here, lanes - 1, 1)
        d_prev[i] = pltpu.roll(here, 1, 1)
        bend = pltpu.roll(skew[i].astype(jnp.float32), 2 * i, 1)
        step = inverse((0.5 * ratio_x) * (here + before))
        rho[i] = step
        a = a + step * c
        b = b + step * d
        return (a, b, c + a, d + b, here, jnp.where(owner == i, bend, acc))

    lead = d_pad[0, 8 : 8 + rows, :]
    a, b, c, d, last, acc = lax.fori_loop(
        0, planes, homogeneous, (ones, zeros, zeros, ones, lead, zeros), unroll=4
    )
    skew_edge[...] = acc

    @pl.when(gx > 0)
    def _():
        x_copy.wait_recv()

    step = inverse((0.5 * ratio_x) * (lead + x_halo[...]))
    change = step - rho[0]
    rho[0] = step
    b = b + a * change
    d = d + c * change
    closing = jnp.where(gx == nx - 1, inverse((0.5 * ratio_x) * last), 0.0)
    inv_d = inverse(d)
    own = (inv_d, b * inv_d + closing, c * inv_d)

    def post(at, send_buf, recv_buf, values, partner):
        for n, v in enumerate(values):
            send_buf[n] = v
        copy = remote(send_buf, recv_buf, line_send.at[at], line_recv.at[at], partner, gy, gz)
        copy.start()
        return copy

    line = [post(0, map_send.at[0], map_recv.at[0], own, partners[0])]

    for pad in (u_pad, d_pad, u_next, u_prev):
        flat = pad.reshape(planes * pitch, lanes)
        for row in (7, 8 + rows):
            flat[pl.ds(row, planes, stride=pitch), :] = jnp.zeros((planes, lanes), jnp.float32)

    def source(i, carried):
        heat = u_pad[i, 8 : 8 + rows, :]
        diff = d_pad[i, 8 : 8 + rows, :]
        flux_y = (diff + d_pad[i, 9 : 9 + rows, :]) * (u_pad[i, 9 : 9 + rows, :] - heat) - (
            diff + d_pad[i, 7 : 7 + rows, :]
        ) * (heat - u_pad[i, 7 : 7 + rows, :])
        flux_z = (diff + d_next[i]) * (u_next[i, 8 : 8 + rows, :] - heat) - (
            diff + d_prev[i]
        ) * (heat - u_prev[i, 8 : 8 + rows, :])
        mixed = (u_next[i, 9 : 9 + rows, :] - u_next[i, 7 : 7 + rows, :]) - (
            u_prev[i, 9 : 9 + rows, :] - u_prev[i, 7 : 7 + rows, :]
        )
        bend = skew[i].astype(jnp.float32)
        bend_rows[0, pl.ds(i, 1), :] = bend[0:1, :]
        bend_rows[1, pl.ds(i, 1), :] = bend[rows - 1 : rows, :]
        r_buf[i] = (
            heat
            + ((0.5 * ratio_y) * flux_y + (0.5 * ratio_z) * flux_z)
            + ratio_mix * bend * mixed
        )
        return carried

    lax.fori_loop(0, planes, source, zero, unroll=2)

    flags = [(gx // (1 << s)) % 2 == 1 for s in range(stages)]
    group, right = own, own
    left = (ones, zeros, zeros)
    steps = []
    for s in range(stages - 1):
        if s:
            line.append(post(s, map_send.at[s], map_recv.at[s], group, partners[s]))
        line[s].wait_recv()
        theirs = tuple(map_recv[s, n] for n in range(3))
        first = pick(flags[s], theirs, group)
        second = pick(flags[s], group, theirs)
        joined, weights = link(first, second)
        left_joined, left_weights = link(theirs, left)
        right_joined, right_weights = link(right, theirs)
        steps.append((theirs, first, second, weights, left, left_weights, right, right_weights))
        group = joined
        left = pick(flags[s], left_joined, left)
        right = pick(flags[s], right, right_joined)
    in_right = flags[-1]
    end_weight = group[0] * inverse(group[1])
    line.append(post(
        stages - 1, rel_send.at[0], rel_recv.at[0],
        (jnp.where(in_right, group[2] + group[0] * end_weight, group[1]),), partners[-1],
    ))

    @pl.when(gy > 0)
    def _():
        for copy in down_copy:
            copy.wait_recv()
        down_corner.wait_recv()

    @pl.when(gy < ny - 1)
    def _():
        for copy in up_copy:
            copy.wait_recv()
        up_corner.wait_recv()

    z_copy.wait_recv()
    long_lane = lax.broadcasted_iota(jnp.int32, (planes, lanes), 1)
    r_flat = r_buf.reshape(planes * rows, lanes)
    for way, row, sign in ((0, 0, -ratio_mix), (1, rows - 1, ratio_mix)):
        heat, diff = y_send[way, 0], y_send[way, 1]
        halo, halo_diff = y_recv[way, 0], y_recv[way, 1]
        bend = jnp.where(long_lane == lanes - 1, 0.0, pltpu.roll(halo, lanes - 1, 1)) - jnp.where(
            long_lane == 0, 0.0, pltpu.roll(halo, 1, 1)
        )
        at = pl.ds(row, planes, stride=rows)
        r_flat[at, :] += (0.5 * ratio_y) * (
            diff * halo + halo_diff * (halo - heat)
        ) + sign * bend_rows[way] * bend

    even = lax.rem(lane, jnp.int32(2)) == 0

    def across(x):
        return jnp.where(even, pltpu.roll(x, 1, 1), pltpu.roll(x, lanes - 1, 1))

    own_edge[0:8, :] = jnp.zeros((8, lanes), jnp.float32)
    own_edge[8 : 8 + rows, :] = z_send[0]
    own_edge[8 + rows : 16 + rows, :] = jnp.zeros((8, lanes), jnp.float32)
    heat, diff = z_send[0], z_send[1]
    near = jnp.where(even, 1.0, 0.0)
    near = jnp.where(gz == 0, 1.0 - near, near)
    met_heat = near * across(z_recv[0, 8 : 8 + rows, :])
    met_diff = near * across(z_recv[1, 8 : 8 + rows, :])
    met_bend = near * across(z_recv[0, 9 : 9 + rows, :] - z_recv[0, 7 : 7 + rows, :])
    wrap_bend = across(own_edge[9 : 9 + rows, :] - own_edge[7 : 7 + rows, :])
    edge_term = (0.5 * ratio_z) * (
        (diff + met_diff) * (met_heat - heat) - (diff + across(diff)) * (across(heat) - heat)
    ) + jnp.where(even, -ratio_mix, ratio_mix) * skew_edge[...] * (met_bend - wrap_bend)

    edge_lane = (lane == 0) | (lane == lanes - 1)

    def unpacked(i):
        return pltpu.roll(edge_term, lax.rem(2 * (lanes - i), lanes), 1)

    def particular(i, state):
        wp, fp, extra = state
        side = r_buf[i] + jnp.where(edge_lane, extra, 0.0)
        r_buf[i] = side
        wp = wp + rho[i] * fp
        return (wp, fp + (wp - side), unpacked(i + 1))

    wp, fp, _ = lax.fori_loop(0, planes, particular, (zeros, zeros, unpacked(0)), unroll=4)

    group_pq = (wp - b * inv_d * fp, fp * inv_d)
    left_pq, right_pq = (zeros, zeros), group_pq
    for s in range(stages - 1):
        copy = post(stages + s, pq_send.at[s], pq_recv.at[s], group_pq, partners[s])
        line.append(copy)
        theirs_map, first, second, weights, left_map, left_weights, right_map, right_weights = steps[s]
        copy.wait_recv()
        theirs = tuple(pq_recv[s, n] for n in range(2))
        first_pq = pick(flags[s], theirs, group_pq)
        second_pq = pick(flags[s], group_pq, theirs)
        left_pq = pick(
            flags[s], link_sides(left_weights, theirs_map, theirs, left_map, left_pq), left_pq
        )
        right_pq = pick(
            flags[s], right_pq, link_sides(right_weights, right_map, right_pq, theirs_map, theirs)
        )
        group_pq = link_sides(weights, first, first_pq, second, second_pq)
    copy = post(
        2 * stages - 1, rel_send.at[1], rel_recv.at[1],
        (jnp.where(in_right, group_pq[1] + end_weight * group_pq[0], group_pq[0]),), partners[-1],
    )
    line.append(copy)
    line[stages - 1].wait_recv()
    met = rel_recv[0, 0]
    z0 = jnp.where(in_right, met, 0.0)
    c0 = jnp.where(in_right, 0.0, met)
    left_in = left[0] * inverse(1.0 + z0 * left[2])
    z_in = left[1] + left_in * left[0] * z0
    right_in = right[0] * inverse(jnp.where(in_right, right[1], 1.0 + right[1] * c0))
    c_in = right[2] + right_in * jnp.where(in_right, right[0], right[0] * c0)
    inv_sum = inverse(1.0 + z_in * c_in)
    copy.wait_recv()
    met = rel_recv[1, 0]
    e0 = jnp.where(in_right, met, 0.0)
    e_in = left_pq[0] + left_in * (e0 - z0 * left_pq[1])
    q_in = right_pq[1] + right_in * jnp.where(in_right, right_pq[0], met + c0 * right_pq[0])
    value = (e_in - z_in * q_in) * inv_sum
    flux = -(c_in * e_in + q_in) * inv_sum

    start[0] = value
    start[1] = flux

    for copy in line:
        copy.wait_send()
    z_copy.wait_send()

    @pl.when(gx < nx - 1)
    def _():
        x_copy.wait_send()

    @pl.when(gy > 0)
    def _():
        for copy in up_copy:
            copy.wait_send()
        up_corner.wait_send()

    @pl.when(gy < ny - 1)
    def _():
        for copy in down_copy:
            copy.wait_send()
        down_corner.wait_send()


def march_kernel(r_buf, rho, start, r_hbm, w_hbm, w_buf, store_sem):
    planes = r_buf.shape[0]
    r_store = pltpu.make_async_copy(r_buf, r_hbm, store_sem.at[0])
    r_store.start()

    def march(i, state):
        value, flux = state
        value = value + rho[i] * flux
        w_buf[i] = value
        return (value, flux + (value - r_buf[i]))

    chunks = 4
    size = planes // chunks

    def store(n):
        part = pl.ds(n * size, size)
        return pltpu.make_async_copy(w_buf.at[part], w_hbm.at[part], store_sem.at[1 + n])

    def chunk(n, state):
        state = lax.fori_loop(0, size, lambda i, s: march(n * size + i, s), state, unroll=8)
        store(n).start()
        return state

    lax.fori_loop(0, chunks, chunk, (start[0], start[1]))
    r_store.wait()
    for n in range(chunks):
        store(n).wait()


def body(nx, ny, nz, initial_thermal_state, thermal_spread_rate, yz_skew_factor):
    planes, rows, lanes = initial_thermal_state.shape
    stages = int(math.log2(nx))
    f32 = jnp.float32
    block = jax.ShapeDtypeStruct((planes, rows, lanes), f32)
    padded = pltpu.VMEM((planes, rows + 16, lanes), f32)
    full = pltpu.VMEM((planes, rows, lanes), f32)
    plane = pltpu.VMEM((rows, lanes), f32)
    faces = pltpu.VMEM((2, 2, planes, lanes), f32)
    maps = pltpu.VMEM((stages - 1, 3, rows, lanes), f32)
    sides = pltpu.VMEM((stages - 1, 2, rows, lanes), f32)
    relation = pltpu.VMEM((2, 1, rows, lanes), f32)
    r, rho, start = pl.pallas_call(
        functools.partial(kernel, nx, ny, nz),
        out_shape=(full, full, pltpu.VMEM((2, rows, lanes), f32)),
        in_specs=[pl.BlockSpec(memory_space=pltpu.HBM)] * 3,
        out_specs=(pl.BlockSpec(memory_space=pltpu.VMEM),) * 3,
        scratch_shapes=[
            padded, padded, padded, padded, full, full,
            pltpu.VMEM((planes, rows, lanes), jnp.bfloat16),
            plane, faces, faces, pltpu.VMEM((2, rows, lanes), f32), pltpu.VMEM((2, rows + 16, lanes), f32),
            pltpu.VMEM((rows + 16, lanes), f32), plane, pltpu.VMEM((2, planes, lanes), f32),
            maps, maps, sides, sides, relation, relation,
            pltpu.SemaphoreType.DMA((3,)),
            pltpu.SemaphoreType.DMA((8,)),
            pltpu.SemaphoreType.DMA((8,)),
            pltpu.SemaphoreType.DMA((2 * stages,)),
            pltpu.SemaphoreType.DMA((2 * stages,)),
        ],
        compiler_params=pltpu.CompilerParams(
            collective_id=0, has_side_effects=True, vmem_limit_bytes=VMEM1
        ),
    )(initial_thermal_state, thermal_spread_rate, yz_skew_factor)
    return pl.pallas_call(
        march_kernel,
        out_shape=(block, block),
        in_specs=[pl.BlockSpec(memory_space=pltpu.VMEM)] * 3,
        out_specs=(pl.BlockSpec(memory_space=pl.ANY),) * 2,
        scratch_shapes=[full, pltpu.SemaphoreType.DMA((5,))],
        compiler_params=pltpu.CompilerParams(vmem_limit_bytes=VMEM2),
    )(r, rho, start)


def solution(mesh):
    shape = dict(mesh.shape)
    spec = P("gx", "gy", "gz")
    return jax.shard_map(
        functools.partial(body, shape["gx"], shape["gy"], shape["gz"]),
        mesh=mesh, in_specs=(spec,) * 3, out_specs=(spec,) * 2, check_vma=False,
    )
```

profile of v0, /device:TPU:0, one launch (start us, length us, event | category | flops | bytes accessed | tf_op | source)
XLA Modules:
  0.0 16.7 jit_solution(9435476824229838891)
XLA Ops:
  0.6 14.7 %shard_map.50 = (f32[64,32,128]{2,1,0:T(8,128)S(1)}, f32[64,32,128]{2,1,0:T(8,128)S(1)}, f32[2,32,128]{2,1,0:T(8,128)S(1)}) custom-call(f32[64,32,128]{2,1,0:T(8,128)} %u_hbm.1, f32[64,32,128]{2,1,0:T(8,128)} %d_hbm.1, bf16[64,32,128]{2,1,0:T(8,128)(2,1)} %k_hbm.1), custom_call_target="tpu_custom_call" | custom-call | tf_op jit(solution)/shard_map/pallas_call | solution.py:455
  15.3 1.4 %shard_map.51 = (f32[64,32,128]{2,1,0:T(8,128)}, f32[64,32,128]{2,1,0:T(8,128)}) custom-call(f32[64,32,128]{2,1,0:T(8,128)S(1)} %get-tuple-element.5.r_buf, f32[64,32,128]{2,1,0:T(8,128)S(1)} %get-tuple-element.6.rho, f32[2,32,128]{2,1,0:T(8,128)S(1)} %get-tuple-element.7.start), custom_call_target="tpu_custom_call" | custom-call | tf_op jit(solution)/shard_map/pallas_call | solution.py:476
where the time goes:
time: 16.8 us; the launch traced here: 16.7 us
  Pallas kernels  16 us (95%)
  between operations  0.64 us (4%)
    pallas_call x1, Pallas kernels, body(): pl.pallas_call(functools.partial(kernel, nx, ny, nz), out_shape=(full, fu...  14.7 us
    pallas_call x1, Pallas kernels, body(): pl.pallas_call(march_kernel, out_shape=(block, block), in_specs=[pl.Block...  1.35 us

commit v1 on v0

--- a/solution.py
+++ b/solution.py
@@ -72,7 +72,8 @@
         pl.semaphore_signal(barrier, inc=1, device_id=(x, y, z), device_id_type=MESH)
 
     partners = [gx + (1 << s) - 2 * (1 << s) * ((gx // (1 << s)) % 2) for s in range(stages)]
-    for x in partners:
+    diagonal = partners[-1] + partners[-2] - gx
+    for x in (*partners, diagonal):
         greet(x, gy, gz)
     greet(gx, gy, other_z)
 
@@ -93,7 +94,7 @@
     one = jnp.int32(1)
     zero = jnp.int32(0)
     awaited = (
-        stages + 1
+        stages + 2
         + jnp.where(gx < nx - 1, one, zero)
         + 2 * jnp.where(gy > 0, one, zero)
         + 2 * jnp.where(gy < ny - 1, one, zero)
@@ -276,17 +277,19 @@
         first = pick(flags[s], theirs, group)
         second = pick(flags[s], group, theirs)
         joined, weights = link(first, second)
+        if s == stages - 2:
+            break
         left_joined, left_weights = link(theirs, left)
         right_joined, right_weights = link(right, theirs)
         steps.append((theirs, first, second, weights, left, left_weights, right, right_weights))
         group = joined
         left = pick(flags[s], left_joined, left)
         right = pick(flags[s], right, right_joined)
-    in_right = flags[-1]
-    end_weight = group[0] * inverse(group[1])
+    in_right, is_second = flags[-1], flags[-2]
+    end = joined[2] + joined[0] * joined[0] * inverse(joined[1])
     line.append(post(
         stages - 1, rel_send.at[0], rel_recv.at[0],
-        (jnp.where(in_right, group[2] + group[0] * end_weight, group[1]),), partners[-1],
+        (jnp.where(in_right, end, joined[1]),), partners[-1],
     ))
 
     @pl.when(gy > 0)
@@ -339,6 +342,29 @@
     def unpacked(i):
         return pltpu.roll(edge_term, lax.rem(2 * (lanes - i), lanes), 1)
 
+    line[stages - 1].wait_recv()
+    met = rel_recv[0, 0]
+    z0 = jnp.where(in_right, met, 0.0)
+    c0 = jnp.where(in_right, 0.0, met)
+    t1, z1, c1 = first
+    t2, z2, c2 = second
+    e_first = t1 * inverse(1.0 + z0 * c1)
+    z_mid = z1 + t1 * e_first * z0
+    e_second = t2 * inverse(1.0 + z_mid * c2)
+    q_second = t2 * inverse(jnp.where(in_right, z2, 1.0 + z2 * c0))
+    p_second = jnp.where(in_right, q_second, q_second * c0)
+    c_mid = c2 + t2 * p_second
+    q_first = t1 * inverse(1.0 + z1 * c_mid)
+    p_first = q_first * c_mid
+    z_in = jnp.where(is_second, z_mid, z0)
+    c_in = jnp.where(is_second, c_mid, c1 + t1 * p_first)
+    e_from_q = jnp.where(is_second, e_second, e_first) * z_in
+    q_from_p = jnp.where(is_second, p_second, p_first)
+    to_middle = jnp.where(
+        in_right, jnp.where(is_second, q_first, 1.0), jnp.where(is_second, 1.0, e_second)
+    )
+    inv_sum = inverse(1.0 + z_in * c_in)
+
     def particular(i, state):
         wp, fp, extra = state
         side = r_buf[i] + jnp.where(edge_lane, extra, 0.0)
@@ -350,10 +376,10 @@
 
     group_pq = (wp - b * inv_d * fp, fp * inv_d)
     left_pq, right_pq = (zeros, zeros), group_pq
-    for s in range(stages - 1):
+    for s in range(stages - 2):
         copy = post(stages + s, pq_send.at[s], pq_recv.at[s], group_pq, partners[s])
         line.append(copy)
-        theirs_map, first, second, weights, left_map, left_weights, right_map, right_weights = steps[s]
+        theirs_map, one_map, two_map, weights, left_map, left_weights, right_map, right_weights = steps[s]
         copy.wait_recv()
         theirs = tuple(pq_recv[s, n] for n in range(2))
         first_pq = pick(flags[s], theirs, group_pq)
@@ -364,26 +390,44 @@
         right_pq = pick(
             flags[s], right_pq, link_sides(right_weights, right_map, right_pq, theirs_map, theirs)
         )
-        group_pq = link_sides(weights, first, first_pq, second, second_pq)
-    copy = post(
-        2 * stages - 1, rel_send.at[1], rel_recv.at[1],
-        (jnp.where(in_right, group_pq[1] + end_weight * group_pq[0], group_pq[0]),), partners[-1],
-    )
-    line.append(copy)
-    line[stages - 1].wait_recv()
-    met = rel_recv[0, 0]
-    z0 = jnp.where(in_right, met, 0.0)
-    c0 = jnp.where(in_right, 0.0, met)
-    left_in = left[0] * inverse(1.0 + z0 * left[2])
-    z_in = left[1] + left_in * left[0] * z0
-    right_in = right[0] * inverse(jnp.where(in_right, right[1], 1.0 + right[1] * c0))
-    c_in = right[2] + right_in * jnp.where(in_right, right[0], right[0] * c0)
-    inv_sum = inverse(1.0 + z_in * c_in)
-    copy.wait_recv()
+        group_pq = link_sides(weights, one_map, first_pq, two_map, second_pq)
+    e_part = group_pq[0] - e_from_q * group_pq[1]
+    q_part = group_pq[1] + q_from_p * group_pq[0]
+    at = 2 * stages - 2
+    rel_send[2, 0] = jnp.where(in_right, q_part, e_part) * to_middle
+    for n, partner in enumerate((diagonal, partners[-1])):
+        copy = remote(
+            rel_send.at[2], rel_recv.at[2 + n], line_send.at[at + n], line_recv.at[at + n],
+            partner, gy, gz,
+        )
+        copy.start()
+        line.append(copy)
+    pair = post(
+        at + 2, rel_send.at[1], rel_recv.at[1],
+        (jnp.where(is_second, q_part, e_part),), partners[-2],
+    )
+    pair.wait_recv()
     met = rel_recv[1, 0]
-    e0 = jnp.where(in_right, met, 0.0)
-    e_in = left_pq[0] + left_in * (e0 - z0 * left_pq[1])
-    q_in = right_pq[1] + right_in * jnp.where(in_right, right_pq[0], met + c0 * right_pq[0])
+    for copy in line[-2:]:
+        copy.wait_recv()
+    line.append(pair)
+    middle = rel_recv[2, 0] + rel_recv[3, 0]
+    e0 = jnp.where(in_right, middle, 0.0)
+    q0 = jnp.where(in_right, 0.0, middle)
+    e_in = jnp.where(is_second, met + e_first * e0, e0)
+    q_mid = jnp.where(is_second, q_part, met) + q_second * q0
+    q_in = jnp.where(is_second, q_mid, q_part + q_first * q_mid)
+    if stages > 2:
+        last_one = in_right & is_second
+        c_end = jnp.where(is_second, c0, c_mid)
+        q_end = jnp.where(is_second, q0, q_mid)
+        share = left[0] * inverse(1.0 + z_in * left[2])
+        e_in = left_pq[0] + share * (e_in - z_in * left_pq[1])
+        z_in = left[1] + share * left[0] * z_in
+        share = right[0] * inverse(jnp.where(last_one, right[1], 1.0 + right[1] * c_end))
+        c_in = right[2] + right[0] * jnp.where(last_one, share, share * c_end)
+        q_in = right_pq[1] + share * jnp.where(last_one, right_pq[0], q_end + c_end * right_pq[0])
+        inv_sum = inverse(1.0 + z_in * c_in)
     value = (e_in - z_in * q_in) * inv_sum
     flux = -(c_in * e_in + q_in) * inv_sum
 
@@ -451,7 +495,7 @@
     faces = pltpu.VMEM((2, 2, planes, lanes), f32)
     maps = pltpu.VMEM((stages - 1, 3, rows, lanes), f32)
     sides = pltpu.VMEM((stages - 1, 2, rows, lanes), f32)
-    relation = pltpu.VMEM((2, 1, rows, lanes), f32)
+    relation = pltpu.VMEM((4, 1, rows, lanes), f32)
     r, rho, start = pl.pallas_call(
         functools.partial(kernel, nx, ny, nz),
         out_shape=(full, full, pltpu.VMEM((2, rows, lanes), f32)),
@@ -466,8 +510,8 @@
             pltpu.SemaphoreType.DMA((3,)),
             pltpu.SemaphoreType.DMA((8,)),
             pltpu.SemaphoreType.DMA((8,)),
-            pltpu.SemaphoreType.DMA((2 * stages,)),
-            pltpu.SemaphoreType.DMA((2 * stages,)),
+            pltpu.SemaphoreType.DMA((2 * stages + 1,)),
+            pltpu.SemaphoreType.DMA((2 * stages + 1,)),
         ],
         compiler_params=pltpu.CompilerParams(
             collective_id=0, has_side_effects=True, vmem_limit_bytes=VMEM1

time: 16.8 us -> 18.4 us (1.095)
  Pallas kernels: 16 us -> 17.6 us
    pallas_call x1, Pallas kernels: 14.7 us -> 16.2 us  [body(): pl.pallas_call(functools.partial(kernel, nx, ny, nz), out_shape=(full, fu...]
where the time goes in v1:
time: 18.4 us; the launch traced here: 18.2 us
  Pallas kernels  17.6 us (96%)
  between operations  0.64 us (3%)
    pallas_call x1, Pallas kernels, body(): pl.pallas_call(functools.partial(kernel, nx, ny, nz), out_shape=(full, fu...  16.2 us
    pallas_call x1, Pallas kernels, body(): pl.pallas_call(march_kernel, out_shape=(block, block), in_specs=[pl.Block...  1.35 us

profile of v1, /device:TPU:0, one launch (start us, length us, event | category | flops | bytes accessed | tf_op | source)
XLA Modules:
  0.0 18.2 jit_solution(67523188297664376)
XLA Ops:
  0.6 16.2 %shard_map.50 = (f32[64,32,128]{2,1,0:T(8,128)S(1)}, f32[64,32,128]{2,1,0:T(8,128)S(1)}, f32[2,32,128]{2,1,0:T(8,128)S(1)}) custom-call(f32[64,32,128]{2,1,0:T(8,128)} %u_hbm.1, f32[64,32,128]{2,1,0:T(8,128)} %d_hbm.1, bf16[64,32,128]{2,1,0:T(8,128)(2,1)} %k_hbm.1), custom_call_target="tpu_custom_call" | custom-call | tf_op jit(solution)/shard_map/pallas_call | solution.py:499
  16.9 1.4 %shard_map.51 = (f32[64,32,128]{2,1,0:T(8,128)}, f32[64,32,128]{2,1,0:T(8,128)}) custom-call(f32[64,32,128]{2,1,0:T(8,128)S(1)} %get-tuple-element.5.r_buf, f32[64,32,128]{2,1,0:T(8,128)S(1)} %get-tuple-element.6.rho, f32[2,32,128]{2,1,0:T(8,128)S(1)} %get-tuple-element.7.start), custom_call_target="tpu_custom_call" | custom-call | tf_op jit(solution)/shard_map/pallas_call | solution.py:520
